TPU v7x, 256 devices: a whole 4x4x8 slice. The times are simulated.
256 devices in a mesh: pos: 16 (over z, x_hi), var: 16 (over x_lo, y, core).
Axes of the slice: x: 4 (x_hi: 2, x_lo: 2; x = x_hi * 2 + x_lo), y: 4, z: 8, core: 2. Of those that a mesh axis runs over, the one named last changes fastest.
Arguments:
- tower_input: bfloat16 [1024, 1536], P('pos', 'var'), may hold values from -11 to 11
- var_bins: int32 [2048], P(('pos', 'var')), may hold values from 0 to 1023, as said below
- alt_codes: int32 [2048], P(('pos', 'var')), may hold values from 0 to 3
- dilations: int32 [2], replicated, may hold values from 1 to 7, as said below
- base_embed: float32 [4, 1536], replicated, may hold values from -6 to 6
- dw_kernel: float32 [2, 3, 1536], replicated, may hold values from -3 to 3
- norm_gain: float32 [2, 1536], replicated, may hold values from 0.25 to 1.75
- pw_weight: bfloat16 [2, 1536, 1536], replicated, may hold values from -0.15625 to 0.15625
Outputs:
- effects: float32 [2048, 1536], P(('pos', 'var'))
Inputs may be any that keep to these rules, and one draw needn't show every extreme that they name: `var_bins`: variant bins cluster around a few centres of the locus. One of the two dilations is 7.
All inputs are finite; a program needn't handle non-finite values.
Results may differ from a plain program's by a relative error of at most 0.004.
The roundings to bfloat16 on the way count: a program that leaves them out, or rounds other values in their place, can miss the bound.
Values may be sent and summed in bfloat16 or wider, within the bound.
A program may use at most 64 MiB of HBM per device.

v0:
```python
import jax
import jax.numpy as jnp
from jax import lax
from jax.sharding import PartitionSpec as P

DMAX = 7
CONE = 32


def padded_2(cells, sides, width):
    for axis, dim in sides:
        count = lax.axis_size(axis)
        ends = count - 1
        head = lax.slice_in_dim(cells, 0, width, axis=dim)
        tail = lax.slice_in_dim(cells, cells.shape[dim] - width, cells.shape[dim], axis=dim)
        cells = jnp.concatenate(
            [
                lax.ppermute(tail, axis, [(i, (i + 1) % count) for i in range(ends)]),
                cells,
                lax.ppermute(head, axis, [((i + 1) % count, i) for i in range(ends)]),
            ],
            axis=dim,
        )
    return cells


def layer_block(window, start, count, dilation, taps, gain, weight):
    values = window.astype(jnp.float32)
    left = lax.dynamic_slice_in_dim(values, start - dilation, count, 1)
    middle = values[:, start : start + count]
    right = lax.dynamic_slice_in_dim(values, start + dilation, count, 1)
    conv = taps[0] * left + taps[1] * middle + taps[2] * right
    meansq = jnp.mean(conv * conv, axis=-1, keepdims=True)
    normed = conv * lax.rsqrt(meansq + 1e-06) * gain
    feature = jax.nn.gelu(normed).astype(jnp.bfloat16)
    batch, rows, chans = feature.shape
    proj = jnp.dot(feature.reshape(batch * rows, chans), weight, preferred_element_type=jnp.float32)
    return middle + proj.reshape(batch, rows, weight.shape[1])


def cone_effect(
    in_window,
    one_window,
    bins,
    codes,
    dilations,
    taps_one,
    taps_two,
    norm_gain,
    pw_weight,
    base_embed,
    total_bins,
):
    outer = CONE + DMAX + 1
    half = CONE // 2
    onehot = (codes[:, None] == jnp.arange(4, dtype=jnp.int32)[None, :]).astype(jnp.float32)
    change = jnp.dot(onehot, base_embed, precision=lax.Precision.HIGHEST)
    marker = (jnp.arange(in_window.shape[1], dtype=jnp.int32) == outer).astype(jnp.float32)
    alt_zero = in_window.astype(jnp.float32) + marker[None, :, None] * change[:, None, :]
    alt_one = layer_block(
        alt_zero, outer - half, CONE, dilations[0], taps_one, norm_gain[0], pw_weight[0]
    )
    cone_rows = bins[:, None] - half + jnp.arange(CONE, dtype=jnp.int32)[None, :]
    inside = ((cone_rows >= 0) & (cone_rows < total_bins)).astype(jnp.float32)[..., None]
    alt_one = (alt_one * inside).astype(jnp.bfloat16)
    alt_field = jnp.concatenate(
        [one_window[:, : CONE - half], alt_one, one_window[:, 2 * CONE - half :]], axis=1
    )
    alt_two = layer_block(
        alt_field, CONE - half, CONE, dilations[1], taps_two, norm_gain[1], pw_weight[1]
    )
    base_two = layer_block(
        one_window, CONE - half, CONE, dilations[1], taps_two, norm_gain[1], pw_weight[1]
    )
    return jnp.sum((alt_two - base_two) * inside, axis=1)


def local(tower_input, var_bins, alt_codes, dilations, base_embed, dw_kernel, norm_gain, pw_weight):
    outer = CONE + DMAX + 1
    block_bins, width = tower_input.shape
    channels = pw_weight.shape[1]
    strand_taps = [(dw_kernel[0], dw_kernel[1]), (dw_kernel[0][::-1], dw_kernel[1][::-1])]
    first_col = lax.axis_index("var") * width
    padded = padded_2(tower_input, (("pos", 0),), DMAX)
    own_gain = lax.dynamic_slice_in_dim(norm_gain[0], first_col, width, 0)
    convs = []
    for taps_one, taps_two in strand_taps:
        own_taps = lax.dynamic_slice_in_dim(taps_one, first_col, width, 1)
        values = padded.astype(jnp.float32)
        left = lax.dynamic_slice_in_dim(values, DMAX - dilations[0], block_bins, 0)
        right = lax.dynamic_slice_in_dim(values, DMAX + dilations[0], block_bins, 0)
        convs.append(
            own_taps[0] * left
            + own_taps[1] * values[DMAX : DMAX + block_bins]
            + own_taps[2] * right
        )
    stacked = jnp.stack(convs)
    squares = lax.psum(jnp.sum(stacked * stacked, axis=-1), "var")
    normed = stacked * lax.rsqrt(squares / channels + 1e-06)[..., None] * own_gain
    feature = jax.nn.gelu(normed).astype(jnp.bfloat16).reshape(2 * block_bins, width)
    own_weight = lax.dynamic_slice_in_dim(pw_weight[0], first_col, width, 1)
    proj = jnp.dot(
        lax.all_gather(feature, "var", axis=1, tiled=True),
        own_weight,
        preferred_element_type=jnp.float32,
    )
    layer_one = (tower_input.astype(jnp.float32)[None] + proj.reshape(2, block_bins, width)).astype(
        jnp.bfloat16
    )
    wide = (
        lax.all_gather(tower_input, "var", axis=1, tiled=True),
        lax.all_gather(layer_one[0], "var", axis=1, tiled=True),
        lax.all_gather(layer_one[1], "var", axis=1, tiled=True),
    )
    full_in, full_fwd, full_rev = (
        lax.all_gather(wide[0], "pos", axis=0, tiled=True),
        lax.all_gather(wide[1], "pos", axis=0, tiled=True),
        lax.all_gather(wide[2], "pos", axis=0, tiled=True),
    )
    total_bins = full_in.shape[0]
    in_padded = jnp.pad(full_in, ((outer, outer), (0, 0)))
    in_window = jax.vmap(lambda start: lax.dynamic_slice_in_dim(in_padded, start, 2 * outer, 0))(
        var_bins
    )
    one_windows = []
    for strand_first in (full_fwd, full_rev):
        one_padded = jnp.pad(strand_first, ((CONE, CONE), (0, 0)))
        one_windows.append(
            jax.vmap(lambda start: lax.dynamic_slice_in_dim(one_padded, start, 2 * CONE, 0))(
                var_bins
            )
        )
    total = jnp.zeros((var_bins.shape[0], channels), jnp.float32)
    for strand in range(2):
        strand_codes = alt_codes if strand == 0 else 3 - alt_codes
        taps_one, taps_two = strand_taps[strand]
        total = total + cone_effect(
            in_window,
            one_windows[strand],
            var_bins,
            strand_codes,
            dilations,
            taps_one,
            taps_two,
            norm_gain,
            pw_weight,
            base_embed,
            total_bins,
        )
    return total * (0.5 / CONE)


def solution(mesh):
    in_specs = (P("pos", "var"), P(("pos", "var")), P(("pos", "var")), P(), P(), P(), P(), P())
    out_specs = P(("pos", "var"), None)
    return jax.shard_map(local, mesh=mesh, in_specs=in_specs, out_specs=out_specs, check_vma=False)
```

profile of v0, /device:TPU:1, one launch (start us, length us, event | category | flops | bytes accessed | tf_op | source)
XLA Modules:
  0.0 358.1 jit_solution(18228609920980008300)
XLA Ops:
  6.6 22.2 %all-gather.4 = bf16[16,96,64]{1,2,0:T(8,128)(2,1)S(1)} all-gather(bf16[1,96,64]{1,2,0:T(8,128)(2,1)} %bitcast.133), channel_id=1, replica_groups=mesh['pos'=16,'var'=16] {'var'}, dimensions={0}, use_global_device_ids=true | all-gather | bytes 208896 | tf_op jit(solution)/shard_map/all_gather | solution.py:111
  30.6 4.3 %collective-permute-start = (bf16[7,96]{1,0:T(8,128)(2,1)S(1)}, bf16[7,96]{1,0:T(8,128)(2,1)S(1)}, u32[]{:S(2)}, u32[]{:S(2)}) collective-permute-start(bf16[7,96]{1,0:T(8,128)(2,1)S(1)} %get-tuple-element.104), channel_id=1, source_target_pairs={{0,16},{16,32},{32,48},{48,64},{64,80},{80,96},{96,112},{112,128},... | collective-permute-start | bytes 4040 | tf_op jit(solution)/shard_map/ppermute | solution.py:18
  41.4 4.9 %slice.181 = bf16[1,1536,1536]{2,1,0:T(8,128)(2,1)} slice(bf16[2,1536,1536]{2,1,0:T(8,128)(2,1)} %param.15), slice={[0:1], [0:1536], [0:1536]} | slice | bytes 9437184 | tf_op jit(solution)/shard_map/slice | solution.py:101
  46.4 26.9 %psum.7 = f32[2,64]{1,0:T(2,128)S(1)} all-reduce(f32[2,64]{1,0:T(2,128)S(1)} %get-tuple-element.87), channel_id=1, replica_groups=mesh['pos'=16,'var'=16] {'var'}, use_global_device_ids=true, to_apply=%region_1.0 | all-reduce | flops 128 | bytes 1024 | tf_op jit(solution)/shard_map/psum | solution.py:98
  73.7 18.6 %all_gather.21 = bf16[128,1536]{0,1:T(8,128)(2,1)S(1)} all-gather(bf16[128,96]{0,1:T(8,128)(2,1)S(1)} %fusion.164), channel_id=1, replica_groups=mesh['pos'=16,'var'=16] {'var'}, dimensions={1}, use_global_device_ids=true | all-gather | bytes 417792 | tf_op jit(solution)/shard_map/all_gather | solution.py:103
  94.1 20.6 %all-gather = bf16[1,64,1536]{1,0,2:T(2,128)(2,1)S(1)} all-gather(bf16[1,64,96]{1,0,2:T(2,128)(2,1)S(1)} %copy.31), channel_id=2, replica_groups=mesh['pos'=16,'var'=16] {'var'}, dimensions={2}, use_global_device_ids=true | all-gather | bytes 208896 | tf_op jit(solution)/shard_map/all_gather | solution.py:112
  123.8 20.1 %all-gather.2 = bf16[1,64,1536]{1,0,2:T(2,128)(2,1)S(1)} all-gather(bf16[1,64,96]{1,0,2:T(2,128)(2,1)S(1)} %copy.34), channel_id=4, replica_groups=mesh['pos'=16,'var'=16] {'var'}, dimensions={2}, use_global_device_ids=true | all-gather | bytes 208896 | tf_op jit(solution)/shard_map/all_gather | solution.py:113
  147.7 15.8 %while.4 = (s32[]{:T(128)}, bf16[1104,1536]{1,0:T(8,128)(2,1)S(1)}, s32[8,2]{0,1:T(2,128)S(1)}, bf16[8,80,1536]{2,1,0:T(8,128)(2,1)}, s32[]{:T(128)}) while((s32[]{:T(128)}, bf16[1104,1536]{1,0:T(8,128)(2,1)S(1)}, s32[8,2]{0,1:T(2,128)S(1)}, bf16[8,80,1536]{2,1,0:T(8,128)(2,1)}, s32[]{:T(128)}) %tuple.79), condition=%wide.while_cond.1, body=%wide.while_body.1.sunk | while | flops 2 | bytes 492133 | solution.py:122
  163.5 2.9 convert_add_fusion
  168.3 2.5 fusion.55
  170.8 2.5 fusion.52
  173.4 40.0 %all-gather.11.cloned.1.call-done = bf16[1,1024,1536]{2,1,0:T(8,128)(2,1)} async-done(((bf16[1,64,1536]{2,1,0:T(8,128)(2,1)}), bf16[1,1024,1536]{2,1,0:T(8,128)(2,1)}) %all-gather.11.cloned.1.call-update) | async-done | bytes 3145744 | tf_op jit(solution)/shard_map/all_gather | solution.py:117
  213.4 3.8 %pad.13 = bf16[1088,1536]{1,0:T(8,128)(2,1)} pad(bf16[1024,1536]{1,0:T(8,128)(2,1)} %bitcast.124, bf16[]{:T(256)} %constant.78.clone.1), padding=32_32x0_0 | pad | bytes 6488066 | tf_op jit(solution)/shard_map/jit(_pad)/pad | solution.py:127
  217.3 17.8 %while.3 = (s32[]{:T(128)}, bf16[1088,1536]{1,0:T(8,128)(2,1)}, s32[8,2]{0,1:T(2,128)S(1)}, bf16[8,64,1536]{2,1,0:T(8,128)(2,1)S(1)}, s32[]{:T(128)}) while((s32[]{:T(128)}, bf16[1088,1536]{1,0:T(8,128)(2,1)}, s32[8,2]{0,1:T(2,128)S(1)}, bf16[8,64,1536]{2,1,0:T(8,128)(2,1)S(1)}, s32[]{:T(128)}) %tuple.76), condition=%wide.while_cond, body=%wide.while_body.sunk | while | flops 2 | bytes 393321 | solution.py:129
  239.2 66.8 %all-gather.13.cloned.1.call-done = bf16[1,1024,1536]{2,1,0:T(8,128)(2,1)} async-done(((bf16[1,64,1536]{2,1,0:T(8,128)(2,1)}), bf16[1,1024,1536]{2,1,0:T(8,128)(2,1)}) %all-gather.13.cloned.1.call-update) | async-done | bytes 3145744 | tf_op jit(solution)/shard_map/all_gather | solution.py:118
  306.0 3.8 %pad.15 = bf16[1088,1536]{1,0:T(8,128)(2,1)} pad(bf16[1024,1536]{1,0:T(8,128)(2,1)} %bitcast.125, bf16[]{:T(256)} %constant.78.clone.1), padding=32_32x0_0 | pad | bytes 6488066 | tf_op jit(solution)/shard_map/jit(_pad)/pad | solution.py:127
  311.1 23.3 %while.5 = (s32[]{:T(128)}, bf16[1088,1536]{1,0:T(8,128)(2,1)}, s32[8,2]{0,1:T(2,128)S(1)}, bf16[8,64,1536]{2,1,0:T(8,128)(2,1)}, s32[]{:T(128)}) while((s32[]{:T(128)}, bf16[1088,1536]{1,0:T(8,128)(2,1)}, s32[8,2]{0,1:T(2,128)S(1)}, bf16[8,64,1536]{2,1,0:T(8,128)(2,1)}, s32[]{:T(128)}) %tuple.91), condition=%wide.while_cond.2, body=%wide.while_body.2.sunk | while | flops 2 | bytes 393829 | solution.py:129
  317.5 2.3 bitcast_dynamic-update-slice_fusion.8
  320.4 2.3 bitcast_dynamic-update-slice_fusion.8
  323.3 2.3 bitcast_dynamic-update-slice_fusion.8
  329.1 2.3 bitcast_dynamic-update-slice_fusion.8
  332.1 2.3 bitcast_dynamic-update-slice_fusion.8
  339.0 3.4 multiply_reduce_fusion
  342.8 3.1 fusion.22
  (189 shorter events, 78.9 us)
Async XLA Ops:
  6.5 116.8 %copy-start = (f32[4,1536]{1,0:T(4,128)S(1)}, f32[4,1536]{1,0:T(4,128)}, u32[]{:S(2)}) copy-start(f32[4,1536]{1,0:T(4,128)} %param.12) | copy-start | bytes 73732
  6.5 34.8 %copy-start.9 = (bf16[64,96]{1,0:T(8,128)(2,1)S(1)}, bf16[64,96]{1,0:T(8,128)(2,1)}, u32[]{:S(2)}) copy-start(bf16[64,96]{1,0:T(8,128)(2,1)} %param.8) | copy-start | bytes 36868
  6.5 31.1 %copy-start.17 = (s32[2]{0:T(128)S(1)}, s32[2]{0:T(128)}, u32[]{:S(2)}) copy-start(s32[2]{0:T(128)} %param.11) | copy-start | bytes 28
  6.5 31.7 %copy-start.13 = (f32[2,1536]{1,0:T(2,128)S(1)}, f32[2,1536]{1,0:T(2,128)}, u32[]{:S(2)}) copy-start(f32[2,1536]{1,0:T(2,128)} %param.14) | copy-start | bytes 36868
  6.5 139.0 %all-gather.9.cloned.1.call-start = ((), (), s32[]{:S(2)}) async-start(), calls=%async_computation | async-start | bytes 3342336 | tf_op jit(solution)/shard_map/all_gather | solution.py:116
  29.9 183.5 %all-gather.11.cloned.1.call-start = ((), (), s32[]{:S(2)}) async-start(), calls=%async_computation.1 | async-start | bytes 3342336 | tf_op jit(solution)/shard_map/all_gather | solution.py:117
  30.6 15.6 %collective-permute-start = (bf16[7,96]{1,0:T(8,128)(2,1)S(1)}, bf16[7,96]{1,0:T(8,128)(2,1)S(1)}, u32[]{:S(2)}, u32[]{:S(2)}) collective-permute-start(bf16[7,96]{1,0:T(8,128)(2,1)S(1)} %get-tuple-element.104), channel_id=1, source_target_pairs={{0,16},{16,32},{32,48},{48,64},{64,80},{80,96},{96,112},{112,128},... | collective-permute-start | bytes 4040 | tf_op jit(solution)/shard_map/ppermute | solution.py:18
  35.0 11.3 %collective-permute-start.1 = (bf16[7,96]{1,0:T(8,128)(2,1)S(1)}, bf16[7,96]{1,0:T(8,128)(2,1)S(1)}, u32[]{:S(2)}, u32[]{:S(2)}) collective-permute-start(bf16[7,96]{1,0:T(8,128)(2,1)S(1)} %get-tuple-element.105), channel_id=1, source_target_pairs={{16,0},{32,16},{48,32},{64,48},{80,64},{96,80},{112,96},{128,112},... | collective-permute-start | bytes 4040 | tf_op jit(solution)/shard_map/ppermute | solution.py:20
  92.5 28.8 %copy-start.20 = (s32[8]{0:T(128)S(1)}, s32[8]{0:T(128)}, u32[]{:S(2)}) copy-start(s32[8]{0:T(128)} %param.9) | copy-start | bytes 100
  92.5 29.5 %copy-start.10 = (f32[2,3,1536]{2,0,1:T(2,128)S(1)}, f32[2,3,1536]{2,0,1:T(2,128)}, u32[]{:S(2)}) copy-start(f32[2,3,1536]{2,0,1:T(2,128)} %param.13) | copy-start | bytes 110596
  92.5 30.1 %copy-start.18 = (s32[8]{0:T(128)S(1)}, s32[8]{0:T(128)}, u32[]{:S(2)}) copy-start(s32[8]{0:T(128)} %param.10) | copy-start | bytes 100
  116.3 189.6 %all-gather.13.cloned.1.call-start = ((), (), s32[]{:S(2)}) async-start(), calls=%async_computation.2 | async-start | bytes 3342336 | tf_op jit(solution)/shard_map/all_gather | solution.py:118
  147.7 15.8 %copy-start.19 = (f32[80]{0:T(128)S(1)}, f32[80]{0:T(128)}, u32[]{:S(2)}) copy-start(f32[80]{0:T(128)} %compare_convert_fusion) | copy-start | bytes 964
  163.5 2.9 copy-start.11
  163.5 2.9 copy-start.12
  163.5 4.7 %slice-start = ((s8[9437184]{0:T(1024)(128)(4,1)}), s8[4194304]{0:T(1024)(128)(4,1)S(1)}, s32[]{:S(2)}) async-start(s8[9437184]{0:T(1024)(128)(4,1)} %bitcast.126), calls=%async_computation.3 | async-start | bytes 8388608
  163.5 4.7 %slice-start.1 = ((s8[9437184]{0:T(1024)(128)(4,1)}), s8[4194304]{0:T(1024)(128)(4,1)S(1)}, s32[]{:S(2)}) async-start(s8[9437184]{0:T(1024)(128)(4,1)} %bitcast.126), calls=%async_computation.4 | async-start | bytes 8388608
  166.5 1.8 slice-start.2
  236.3 1.9 copy-start.4
  338.5 3.9 %slice-start.3 = ((s8[9437184]{0:T(1024)(128)(4,1)}), s8[4194304]{0:T(1024)(128)(4,1)S(1)}, s32[]{:S(2)}) async-start(s8[9437184]{0:T(1024)(128)(4,1)} %bitcast.128), calls=%async_computation.6 | async-start | bytes 8388608
  338.9 3.5 slice-start.4
  338.9 3.9 %slice-start.5 = ((s8[9437184]{0:T(1024)(128)(4,1)}), s8[1048576]{0:T(1024)(128)(4,1)S(1)}, s32[]{:S(2)}) async-start(s8[9437184]{0:T(1024)(128)(4,1)} %bitcast.128), calls=%async_computation.8 | async-start | bytes 2097152
  339.0 3.9 %copy-start.14 = (f32[1536]{0:T(1024)S(1)}, f32[1536]{0:T(1024)}, u32[]{:S(2)}) copy-start(f32[1536]{0:T(1024)} %get-tuple-element.43) | copy-start | bytes 18436
  349.3 2.4 copy-start.1
  (8 other events, 11.0 us)
Sparse Core Ops, SparseCore 0:
  30.0 90.2 all-gather.8
  122.9 90.4 all-gather.10
  216.0 89.9 all-gather.12
where the time goes:
time: 362 us; the launch traced here: 358 us
  blocking collectives  108 us (30%)
  waiting for transfers between devices  107 us (30%)
  local copies, waits for them, and re-layouts  87.5 us (24%)
  between operations  21 us (6%)
  matrix products  15.1 us (4%)
  other arithmetic  13.3 us (4%)
  starting transfers between devices  5.75 us (2%)
    all_gather x1, waiting for transfers between devices, local(): lax.all_gather(wide[2], 'pos', axis=0, tiled=True)  66.8 us
    gather x72, local copies, waits for them, and re-layouts  56.7 us
    all_gather x1, waiting for transfers between devices, local(): lax.all_gather(wide[1], 'pos', axis=0, tiled=True)  40 us
    psum x1, blocking collectives, local(): squares = lax.psum(jnp.sum(stacked * stacked, axis=-1), 'var')  26.9 us
    all_gather x1, blocking collectives, local(): lax.all_gather(tower_input, 'var', axis=1, tiled=True)  22.2 us
    all_gather x1, blocking collectives, local(): lax.all_gather(layer_one[0], 'var', axis=1, tiled=True)  20.6 us
    all_gather x1, blocking collectives, local(): lax.all_gather(layer_one[1], 'var', axis=1, tiled=True)  20.1 us
    all_gather x1, blocking collectives, local(): lax.all_gather(feature, 'var', axis=1, tiled=True)  18.6 us
  transfers between devices with their start and end apart: 5, of which 2 were waited for; matrix products, arithmetic and copies ran while one was open for 19% of the time, Pallas kernels for 0%

commit v1 on v0

v1 whole, which is shorter than its diff:
```python
import functools

import jax
import jax.numpy as jnp
from jax import lax
from jax.experimental import pallas as pl
from jax.experimental.pallas import tpu as pltpu
from jax.sharding import PartitionSpec as P

DMAX = 7
CONE = 32
VARS = 8
MARGIN = 4 * DMAX
SLABS = 26
MESH = pl.DeviceIdType.MESH


def gelu_of_norm(conv, gain):
    scale = lax.rsqrt(jnp.mean(conv * conv, axis=-1, keepdims=True) + 1e-06)
    normed = conv * scale * gain
    inner = normed * (0.7978845608028654 + (0.7978845608028654 * 0.044715) * (normed * normed))
    half = 0.5 * normed
    return half + half * jnp.tanh(inner)


def pick(scalars, shape):
    row = lax.broadcasted_iota(jnp.int32, shape, len(shape) - 2)
    value = jnp.full(shape, scalars[0], jnp.int32)
    for v in range(1, VARS):
        value = jnp.where(row == v, scalars[v], value)
    return value


def kernel(
    npos,
    nvar,
    bins_ref,
    codes_ref,
    dil_ref,
    tower_ref,
    embed_ref,
    taps_ref,
    gain_ref,
    weight_ref,
    out_ref,
    w_one,
    w_two,
    field,
    padded,
    bins_row,
    bins_all,
    bins_smem,
    stage,
    send,
    recv,
    rows_x,
    feature,
    first,
    w_sem,
    pos_send,
    pos_recv,
    bin_send,
    bin_recv,
    var_send,
    var_recv,
    smem_sem,
):
    block, width = tower_ref.shape
    bins = npos * block
    chans = out_ref.shape[1]
    my_pos = lax.axis_index("pos")
    my_var = lax.axis_index("var")

    load_one = pltpu.make_async_copy(weight_ref.at[0], w_one, w_sem.at[0])
    load_two = pltpu.make_async_copy(weight_ref.at[1], w_two, w_sem.at[1])
    load_one.start()
    load_two.start()

    barrier = pltpu.get_barrier_semaphore()

    @pl.loop(1, npos)
    def _(i):
        pl.semaphore_signal(
            barrier, inc=1, device_id=(lax.rem(my_pos + i, npos), my_var), device_id_type=MESH
        )

    @pl.loop(1, nvar)
    def _(i):
        pl.semaphore_signal(
            barrier, inc=1, device_id=(my_pos, lax.rem(my_var + i, nvar)), device_id_type=MESH
        )

    lane = lax.broadcasted_iota(jnp.int32, (1, 128), 1)
    line = jnp.zeros((1, 128), jnp.int32)
    for v in range(VARS):
        line = jnp.where(lane == v, bins_ref[v], line)
    bins_row[...] = line
    bins_all[pl.ds(my_var, 1), :] = line
    stage[...] = jnp.zeros_like(stage)
    padded[:MARGIN, :] = jnp.zeros((MARGIN, width), jnp.float32)
    padded[MARGIN + bins :, :] = jnp.zeros((MARGIN, width), jnp.float32)
    pl.semaphore_wait(barrier, npos + nvar - 2)

    def bin_copy(to, slot):
        return pltpu.make_async_remote_copy(
            src_ref=bins_row,
            dst_ref=bins_all.at[pl.ds(slot, 1)],
            send_sem=bin_send.at[to],
            recv_sem=bin_recv.at[slot],
            device_id=(my_pos, to),
            device_id_type=MESH,
        )

    def pos_copy(to, slot):
        return pltpu.make_async_remote_copy(
            src_ref=tower_ref,
            dst_ref=field.at[pl.ds(pl.multiple_of(slot * block, block), block)],
            send_sem=pos_send.at[to],
            recv_sem=pos_recv.at[slot],
            device_id=(to, my_var),
            device_id_type=MESH,
        )

    def var_copy(to, slot):
        return pltpu.make_async_remote_copy(
            src_ref=send.at[to],
            dst_ref=recv.at[slot],
            send_sem=var_send.at[to],
            recv_sem=var_recv.at[slot],
            device_id=(my_pos, to),
            device_id_type=MESH,
        )

    @pl.loop(1, nvar)
    def _(i):
        bin_copy(lax.rem(my_var + i, nvar), my_var).start()

    @pl.loop(1, npos)
    def _(i):
        pos_copy(lax.rem(my_pos + i, npos), my_pos).start()

    padded[pl.ds(MARGIN + my_pos * block, block), :] = tower_ref[...].astype(jnp.float32)

    @pl.loop(1, nvar)
    def _(i):
        other = lax.rem(my_var + i, nvar)
        bin_copy(other, other).wait_recv()

    smem_copy = pltpu.make_async_copy(bins_all, bins_smem, smem_sem)
    smem_copy.start()

    @pl.loop(1, npos)
    def _(i):
        other = lax.rem(my_pos + i, npos)
        pos_copy(other, other).wait_recv()
        rows = field[pl.ds(pl.multiple_of(other * block, block), block), :]
        padded[pl.ds(MARGIN + other * block, block), :] = rows.astype(jnp.float32)

    smem_copy.wait()
    d_one, d_two = dil_ref[0], dil_ref[1]
    shifts = [MARGIN + a * d_one + b * d_two for b in range(-2, 3) for a in range(-2, 3)]

    def gather(to):
        for v in range(VARS):
            at = bins_smem[to, v]
            for j, shift in enumerate(shifts):
                stage[j, pl.ds(v, 1), :] = padded[pl.ds(at + shift, 1), :]
        return stage[...].reshape(SLABS * VARS, width).astype(jnp.bfloat16)

    @pl.loop(1, nvar)
    def _(i):
        to = lax.rem(my_var + i, nvar)
        send[to] = gather(to)
        var_copy(to, my_var).start()

    recv[my_var] = gather(my_var)

    shape = (VARS, chans)
    codes = pick([codes_ref[v] for v in range(VARS)], (VARS, 1))
    centre = pick([bins_ref[v] for v in range(VARS)], (VARS, 1))
    changes = []
    for strand in range(2):
        change = jnp.zeros(shape, jnp.float32)
        for code in range(4):
            row = embed_ref[pl.ds(code if strand == 0 else 3 - code, 1), :]
            change = jnp.where(codes == code, row, change)
        changes.append(change)

    @pl.loop(1, nvar)
    def _(i):
        other = lax.rem(my_var + i, nvar)
        var_copy(other, other).wait_recv()

    @pl.loop(0, SLABS // 2)
    def _(q):
        at = pl.ds(pl.multiple_of(q * 16, 16), 16)
        pair = jnp.concatenate([recv[j, at, :] for j in range(nvar)], axis=-1).astype(jnp.float32)
        rows_x[2 * q] = pair[:VARS]
        rows_x[2 * q + 1] = pair[VARS:]

    def taps_of(layer, strand):
        order = (0, 1, 2) if strand == 0 else (2, 1, 0)
        return [taps_ref[layer, pl.ds(t, 1), :] for t in order]

    def put(at, pair):
        where = pl.ds(pl.multiple_of(at * 16, 16), 16)
        feature[where, :] = jnp.concatenate(pair, axis=0).astype(jnp.bfloat16)

    @pl.loop(0, 5)
    def _(b):
        gain = gain_ref[0:1, :]
        for a in range(3):
            pair = []
            for strand in range(2):
                taps = taps_of(0, strand)
                conv = (
                    taps[0] * rows_x[b * 5 + a]
                    + taps[1] * rows_x[b * 5 + a + 1]
                    + taps[2] * rows_x[b * 5 + a + 2]
                )
                pair.append(gelu_of_norm(conv, gain))
            put(b * 3 + a, pair)

    gain = gain_ref[0:1, :]
    for a in range(3):
        pair = []
        for strand in range(2):
            taps = taps_of(0, strand)
            xs = [rows_x[10 + a + t] for t in range(3)]
            xs[2 - a] = xs[2 - a] + changes[strand]
            pair.append(gelu_of_norm(taps[0] * xs[0] + taps[1] * xs[1] + taps[2] * xs[2], gain))
        put(15 + a, pair)

    load_one.wait()

    step = 256 if chans % 256 == 0 else 128

    @pl.loop(0, chans // step)
    def _(n):
        cols = pl.ds(pl.multiple_of(n * step, step), step)
        first[:, cols] = jnp.dot(feature[...], w_one[:, cols], preferred_element_type=jnp.float32)

    def inside(a, b):
        at = centre + (a - 1) * d_one + (b - 2) * d_two
        return (at >= 0) & (at < bins)

    def rounded(value, keep):
        return jnp.where(keep, value, 0.0).astype(jnp.bfloat16).astype(jnp.float32)

    @pl.loop(0, 5)
    def _(b):
        for a in range(3):
            keep = inside(a, b)
            for strand in range(2):
                at = pl.ds(pl.multiple_of((b * 3 + a) * 16 + 8 * strand, 8), 8)
                first[at, :] = rounded(rows_x[b * 5 + a + 1] + first[at, :], keep)

    for a in range(3):
        keep = inside(a, 2)
        for strand in range(2):
            at = pl.ds((15 + a) * 16 + 8 * strand, 8)
            middle = rows_x[11 + a]
            if a == 1:
                middle = middle + changes[strand]
            first[at, :] = rounded(middle + first[at, :], keep)

    same = d_one == d_two
    total = jnp.zeros(shape, jnp.float32)
    moved = jnp.zeros(shape, jnp.float32)
    gain = gain_ref[1:2, :]
    for strand in range(2):
        taps = taps_of(1, strand)

        def ref_at(a, b):
            return first[pl.ds((b * 3 + a) * 16 + 8 * strand, 8), :]

        def new_at(a):
            return first[pl.ds((15 + a) * 16 + 8 * strand, 8), :]

        def alt_at(a, b):
            if b == 2:
                return new_at(a)
            if b > 2 and a + b - 2 <= 2:
                return jnp.where(same, new_at(a + b - 2), ref_at(a, b))
            return ref_at(a, b)

        for a in range(3):
            for b in range(1, 4):
                weight = inside(a, b).astype(jnp.float32)
                if (a, b) in ((1, 1), (1, 2), (2, 1), (2, 2)):
                    weight = jnp.where(same, 0.0, weight)
                olds = [ref_at(a, b + t) for t in (-1, 0, 1)]
                news = [alt_at(a, b + t) for t in (-1, 0, 1)]
                old, new = (
                    gelu_of_norm(taps[0] * r[0] + taps[1] * r[1] + taps[2] * r[2], gain)
                    .astype(jnp.bfloat16)
                    .astype(jnp.float32)
                    for r in (olds, news)
                )
                total = total + weight * (new - old)
                if b >= 2:
                    moved = moved + weight * (news[1] - olds[1])

    high = total.astype(jnp.bfloat16)
    low = (total - high.astype(jnp.float32)).astype(jnp.bfloat16)
    feature[pl.ds(0, 16), :] = jnp.concatenate(
        [high.astype(jnp.float32), low.astype(jnp.float32)], axis=0
    ).astype(jnp.bfloat16)
    out_ref[...] = moved
    load_two.wait()

    @pl.loop(0, chans // step)
    def _(n):
        cols = pl.ds(pl.multiple_of(n * step, step), step)
        both = jnp.dot(
            feature[pl.ds(0, 16), :], w_two[:, cols], preferred_element_type=jnp.float32
        )
        out_ref[:, cols] = (out_ref[:, cols] + (both[:8] + both[8:])) * (0.5 / CONE)

    @pl.loop(1, nvar)
    def _(i):
        other = lax.rem(my_var + i, nvar)
        bin_copy(other, my_var).wait_send()
        var_copy(other, my_var).wait_send()

    @pl.loop(1, npos)
    def _(i):
        pos_copy(lax.rem(my_pos + i, npos), my_pos).wait_send()


def solution(mesh):
    npos, nvar = mesh.shape["pos"], mesh.shape["var"]

    def local(tower, var_bins, alt_codes, dilations, base_embed, dw_kernel, norm_gain, pw_weight):
        block, width = tower.shape
        chans = pw_weight.shape[1]
        bins = npos * block
        smem = pl.BlockSpec(memory_space=pltpu.SMEM)
        vmem = pl.BlockSpec(memory_space=pltpu.VMEM)
        dma = pltpu.SemaphoreType.DMA
        return pl.pallas_call(
            functools.partial(kernel, npos, nvar),
            out_shape=jax.ShapeDtypeStruct((VARS, chans), jnp.float32),
            in_specs=[smem] * 3 + [vmem] * 4 + [pl.BlockSpec(memory_space=pl.ANY)],
            out_specs=vmem,
            scratch_shapes=[
                pltpu.VMEM((chans, chans), jnp.bfloat16),
                pltpu.VMEM((chans, chans), jnp.bfloat16),
                pltpu.VMEM((bins, width), jnp.bfloat16),
                pltpu.VMEM((bins + 2 * MARGIN, width), jnp.float32),
                pltpu.VMEM((1, 128), jnp.int32),
                pltpu.VMEM((nvar, 128), jnp.int32),
                pltpu.SMEM((nvar, 128), jnp.int32),
                pltpu.VMEM((SLABS, VARS, width), jnp.float32),
                pltpu.VMEM((nvar, SLABS * VARS, width), jnp.bfloat16),
                pltpu.VMEM((nvar, SLABS * VARS, width), jnp.bfloat16),
                pltpu.VMEM((SLABS, VARS, chans), jnp.float32),
                pltpu.VMEM((18 * 16, chans), jnp.bfloat16),
                pltpu.VMEM((18 * 16, chans), jnp.float32),
                dma((2,)),
                dma((npos,)),
                dma((npos,)),
                dma((nvar,)),
                dma((nvar,)),
                dma((nvar,)),
                dma((nvar,)),
                dma,
            ],
            compiler_params=pltpu.CompilerParams(
                collective_id=0, has_side_effects=True, vmem_limit_bytes=48 * 1024 * 1024
            ),
        )(var_bins, alt_codes, dilations, tower, base_embed, dw_kernel, norm_gain, pw_weight)

    in_specs = (P("pos", "var"), P(("pos", "var")), P(("pos", "var")), P(), P(), P(), P(), P())
    return jax.shard_map(
        local, mesh=mesh, in_specs=in_specs, out_specs=P(("pos", "var"), None), check_vma=False
    )
```

time: 362 us -> 46.3 us (0.13)
  blocking collectives: 108 us -> 0 us
  waiting for transfers between devices: 107 us -> 0 us
  local copies, waits for them, and re-layouts: 87.5 us -> 5.52 us
  Pallas kernels: 0 us -> 40 us
  between operations: 21 us -> 0.03 us
  matrix products: 15.1 us -> 0 us
  other arithmetic: 13.3 us -> 0 us
  starting transfers between devices: 5.75 us -> 0 us
    all_gather x3 -> x0, waiting for transfers between devices: 107 us -> none  [the longest x1 66.8 us: local(): lax.all_gather(wide[2], 'pos', axis=0, tiled=True)]
    all_gather x4 -> x0, blocking collectives: 81.5 us -> none  [the longest x1 22.2 us: local(): lax.all_gather(tower_input, 'var', axis=1, tiled=True)]
    gather x72 -> x0, local copies, waits for them, and re-layouts: 56.7 us -> none
    pallas_call x0 -> x1, Pallas kernels: none -> 40 us  [local(): pl.pallas_call(functools.partial(kernel, npos, nvar), out_shape=jax.Shape...]
    psum x1 -> x0, blocking collectives: 26.9 us -> none  [local(): squares = lax.psum(jnp.sum(stacked * stacked, axis=-1), 'var')]
    dot_general x9 -> x0, matrix products: 15.1 us -> none  [the longest x6 13.2 us: layer_block(): jnp.dot(feature.reshape(batch * rows, chans), weight, preferred_element_t...]
    slice x11 -> x0, local copies, waits for them, and re-layouts: 10.8 us -> none  [the longest x1 4.92 us: local(): own_weight = lax.dynamic_slice_in_dim(pw_weight[0], first_col, width, 1)]
    pad x3 -> x0, local copies, waits for them, and re-layouts: 9.75 us -> none  [the longest x2 7.63 us: local(): one_padded = jnp.pad(strand_first, ((CONE, CONE), (0, 0)))]
  transfers between devices with their start and end apart: 5 -> 0, of which waited for: 2 -> 0; matrix products, arithmetic and copies ran while one was open for 19% -> 0% of each run, Pallas kernels for 0% -> 0%
where the time goes in v1:
time: 46.3 us; the launch traced here: 45.6 us
  Pallas kernels  40 us (86%)
  local copies, waits for them, and re-layouts  5.52 us (12%)
    pallas_call x1, Pallas kernels, local(): pl.pallas_call(functools.partial(kernel, npos, nvar), out_shape=jax.Shape...  40 us
    unnamed x14, local copies, waits for them, and re-layouts  5.52 us

profile of v1, /device:TPU:1, one launch (start us, length us, event | category | flops | bytes accessed | tf_op | source)
XLA Modules:
  0.0 45.6 jit_solution(9290653643641064986)
XLA Ops:
  0.0 0.8 %copy.9.taps_ref = f32[2,3,1536]{2,1,0:T(4,128)S(1)} copy(f32[2,3,1536]{2,0,1:T(2,128)} %param.13) | data formatting | bytes 73728 | tf_op args[5]
  0.8 0.0 copy-start
  0.8 0.7 %copy-done = f32[4,1536]{1,0:T(4,128)S(1)} copy-done((f32[4,1536]{1,0:T(4,128)S(1)}, f32[4,1536]{1,0:T(4,128)}, u32[]{:S(2)}) %copy-start) | copy-done | bytes 24600
  1.5 0.0 copy-start.1
  1.5 0.7 %copy-done.1 = bf16[64,96]{1,0:T(8,128)(2,1)S(1)} copy-done((bf16[64,96]{1,0:T(8,128)(2,1)S(1)}, bf16[64,96]{1,0:T(8,128)(2,1)}, u32[]{:S(2)}) %copy-start.1) | copy-done | bytes 12312
  2.2 0.0 copy-start.2
  2.2 0.7 %copy-done.2 = f32[2,1536]{1,0:T(2,128)S(1)} copy-done((f32[2,1536]{1,0:T(2,128)S(1)}, f32[2,1536]{1,0:T(2,128)}, u32[]{:S(2)}) %copy-start.2) | copy-done | bytes 12312
  3.0 0.0 copy-start.3
  3.0 0.7 %copy-done.3 = s32[8]{0:T(128)S(1)} copy-done((s32[8]{0:T(128)S(1)}, s32[8]{0:T(128)}, u32[]{:S(2)}) %copy-start.3) | copy-done | bytes 56
  3.6 0.0 copy-start.4
  3.6 0.7 %copy-done.4 = s32[8]{0:T(128)S(1)} copy-done((s32[8]{0:T(128)S(1)}, s32[8]{0:T(128)}, u32[]{:S(2)}) %copy-start.4) | copy-done | bytes 56
  4.3 0.0 copy-start.5
  4.3 0.7 %copy-done.5 = s32[2]{0:T(128)S(1)} copy-done((s32[2]{0:T(128)S(1)}, s32[2]{0:T(128)}, u32[]{:S(2)}) %copy-start.5) | copy-done | bytes 32
  4.9 40.0 %shard_map.82 = f32[8,1536]{1,0:T(8,128)S(1)} custom-call(s32[8]{0:T(128)S(1)} %copy-done.3, s32[8]{0:T(128)S(1)} %copy-done.4, s32[2]{0:T(128)S(1)} %copy-done.5, bf16[64,96]{1,0:T(8,128)(2,1)S(1)} %copy-done.1, f32[4,1536]{1,0:T(4,128)S(1)} %copy-done, f32[2,3,1536]{2,1,0:T(4,128)S(1)} %copy.9.taps_ref, f32[2,1536]{1,0:T(2,128)S(1)} %copy-done.2, ...), custom_call_target="tpu_custom_call" | custom-call | tf_op jit(solution)/shard_map/pallas_call | solution.py:341
  45.0 0.6 %copy.11 = f32[8,1536]{1,0:T(8,128)} copy(f32[8,1536]{1,0:T(8,128)S(1)} %shard_map.82) | data formatting | bytes 98304
Async XLA Ops:
  0.8 0.7 %copy-start = (f32[4,1536]{1,0:T(4,128)S(1)}, f32[4,1536]{1,0:T(4,128)}, u32[]{:S(2)}) copy-start(f32[4,1536]{1,0:T(4,128)} %embed_ref.1) | copy-start | bytes 73732
  1.5 0.7 %copy-start.1 = (bf16[64,96]{1,0:T(8,128)(2,1)S(1)}, bf16[64,96]{1,0:T(8,128)(2,1)}, u32[]{:S(2)}) copy-start(bf16[64,96]{1,0:T(8,128)(2,1)} %tower_ref.1) | copy-start | bytes 36868
  2.2 0.7 %copy-start.2 = (f32[2,1536]{1,0:T(2,128)S(1)}, f32[2,1536]{1,0:T(2,128)}, u32[]{:S(2)}) copy-start(f32[2,1536]{1,0:T(2,128)} %gain_ref.1) | copy-start | bytes 36868
  3.0 0.7 %copy-start.3 = (s32[8]{0:T(128)S(1)}, s32[8]{0:T(128)}, u32[]{:S(2)}) copy-start(s32[8]{0:T(128)} %bins_ref.1) | copy-start | bytes 100
  3.6 0.7 %copy-start.4 = (s32[8]{0:T(128)S(1)}, s32[8]{0:T(128)}, u32[]{:S(2)}) copy-start(s32[8]{0:T(128)} %codes_ref.1) | copy-start | bytes 100
  4.3 0.7 %copy-start.5 = (s32[2]{0:T(128)S(1)}, s32[2]{0:T(128)}, u32[]{:S(2)}) copy-start(s32[2]{0:T(128)} %dil_ref.1) | copy-start | bytes 28

commit v2 on v1

v2 whole, which is shorter than its diff:
```python
import functools

import jax
import jax.numpy as jnp
from jax import lax
from jax.experimental import pallas as pl
from jax.experimental.pallas import tpu as pltpu
from jax.sharding import PartitionSpec as P

DMAX = 7
CONE = 32
VARS = 8
MARGIN = 32
TILES = 4
CUT = 2
MESH = pl.DeviceIdType.MESH
STEP = 512


def gelu_of_norm(conv, gain):
    scale = lax.rsqrt(jnp.mean(conv * conv, axis=-1, keepdims=True) + 1e-06)
    normed = conv * scale * gain
    inner = normed * (0.7978845608028654 + (0.7978845608028654 * 0.044715) * (normed * normed))
    half = 0.5 * normed
    return half + half * jnp.tanh(inner)


def pick(scalars, shape):
    row = lax.broadcasted_iota(jnp.int32, shape, len(shape) - 2)
    value = jnp.full(shape, scalars[0], jnp.int32)
    for v in range(1, VARS):
        value = jnp.where(row == v, scalars[v], value)
    return value


def fold(rows, width, lane):
    return [
        jnp.where(lane < width, rows[k], pltpu.roll(rows[3], width - 32 * k, 1)) for k in range(3)
    ]


def unfold(three, width, lane):
    moved = [pltpu.roll(three[k], 128 - width + 32 * k, 1) for k in range(3)]
    last = jnp.where(lane < 64, moved[1], moved[2])
    return list(three) + [jnp.where(lane < 32, moved[0], last)]


def kernel(
    npos,
    nvar,
    bins_hbm,
    codes_hbm,
    dil_hbm,
    tower_hbm,
    embed_hbm,
    taps_hbm,
    gain_hbm,
    weight_ref,
    out_ref,
    bins_ref,
    codes_ref,
    dil_ref,
    tower_ref,
    embed_ref,
    taps_ref,
    gain_ref,
    w_one,
    w_two,
    packed,
    field,
    padded,
    bins_row,
    bins_all,
    bins_smem,
    stage,
    send,
    recv,
    rows_x,
    feature,
    first,
    in_sem,
    w_sem,
    pos_send,
    pos_recv,
    bin_send,
    bin_recv,
    var_send,
    var_recv,
    smem_sem,
    ready,
):
    block, width = tower_ref.shape
    bins = npos * block
    chans = out_ref.shape[1]
    my_pos = lax.axis_index("pos")
    my_var = lax.axis_index("var")

    pairs = (
        (tower_hbm, tower_ref),
        (bins_hbm, bins_ref),
        (dil_hbm, dil_ref),
        (codes_hbm, codes_ref),
        (embed_hbm, embed_ref),
        (taps_hbm, taps_ref),
        (gain_hbm, gain_ref),
    )
    loads = [pltpu.make_async_copy(s, d, in_sem.at[i]) for i, (s, d) in enumerate(pairs)]
    for load in loads:
        load.start()
    barrier = pltpu.get_barrier_semaphore()

    @pl.loop(my_pos + 1, npos)
    def _(i):
        pl.semaphore_signal(barrier, inc=1, device_id=(i, my_var), device_id_type=MESH)

    @pl.loop(my_var + 1, nvar)
    def _(i):
        pl.semaphore_signal(barrier, inc=1, device_id=(my_pos, i), device_id_type=MESH)

    load_one = pltpu.make_async_copy(weight_ref.at[0], w_one, w_sem.at[0])
    load_two = pltpu.make_async_copy(weight_ref.at[1], w_two, w_sem.at[1])
    load_one.start()
    load_two.start()

    def bin_copy(to, slot):
        return pltpu.make_async_remote_copy(
            src_ref=bins_row,
            dst_ref=bins_all.at[pl.ds(slot, 1)],
            send_sem=bin_send.at[to],
            recv_sem=bin_recv.at[slot],
            device_id=(my_pos, to),
            device_id_type=MESH,
        )

    def pos_copy(to, slot):
        return pltpu.make_async_remote_copy(
            src_ref=packed,
            dst_ref=field.at[slot],
            send_sem=pos_send.at[to],
            recv_sem=pos_recv.at[slot],
            device_id=(to, my_var),
            device_id_type=MESH,
        )

    def var_copy(part, to, slot):
        at = pl.ds(0, CUT * TILES * VARS) if part == 0 else pl.ds(CUT * TILES * VARS, (5 - CUT) * TILES * VARS)
        return pltpu.make_async_remote_copy(
            src_ref=send.at[to, at],
            dst_ref=recv.at[slot, at],
            send_sem=var_send.at[part, to],
            recv_sem=var_recv.at[part, slot],
            device_id=(my_pos, to),
            device_id_type=MESH,
        )

    wide_lane = lax.broadcasted_iota(jnp.int32, (VARS, 128), 1)
    two_lane = lax.broadcasted_iota(jnp.int32, (16, 128), 1)
    loads[0].wait()
    own = jnp.concatenate(
        [tower_ref[...].astype(jnp.float32), jnp.zeros((block, 128 - width), jnp.float32)], axis=-1
    )
    quarter = block // 4
    folded = fold([own[quarter * k : quarter * (k + 1)] for k in range(4)], width, two_lane)
    packed[...] = jnp.concatenate(folded, axis=0).astype(jnp.bfloat16)
    loads[1].wait()
    lane = lax.broadcasted_iota(jnp.int32, (1, 128), 1)
    line = jnp.zeros((1, 128), jnp.int32)
    for v in range(VARS):
        line = jnp.where(lane == v, bins_ref[v], line)
    bins_row[...] = line
    bins_all[pl.ds(my_var, 1), :] = line

    @pl.when(my_pos + my_var > 0)
    def _():
        pl.semaphore_wait(barrier, my_pos + my_var)

    @pl.loop(0, my_pos)
    def _(i):
        pl.semaphore_signal(ready.at[my_pos], inc=1, device_id=(i, my_var), device_id_type=MESH)

    @pl.loop(0, my_pos)
    def _(i):
        pos_copy(i, my_pos).start()

    @pl.loop(0, my_var)
    def _(i):
        bin_copy(i, my_var).start()

    padded[:MARGIN, :] = jnp.zeros((MARGIN, 128), jnp.float32)
    padded[MARGIN + bins :, :] = jnp.zeros((MARGIN, 128), jnp.float32)
    padded[pl.ds(pl.multiple_of(MARGIN + my_pos * block, 8), block), :] = own

    def keep_block(i):
        three = field[i].astype(jnp.float32)
        four = unfold([three[quarter * k : quarter * (k + 1)] for k in range(3)], width, two_lane)
        for k in range(4):
            at = pl.multiple_of(MARGIN + i * block + quarter * k, 8)
            padded[pl.ds(at, quarter), :] = four[k]

    loads[2].wait()

    @pl.loop(my_var + 1, nvar)
    def _(i):
        bin_copy(i, i).wait_recv()
        bin_copy(i, my_var).start()

    @pl.loop(my_pos + 1, npos)
    def _(i):
        pl.semaphore_wait(ready.at[i], 1)
        pos_copy(i, my_pos).start()

    @pl.loop(0, my_var)
    def _(i):
        bin_copy(i, i).wait_recv()

    smem_copy = pltpu.make_async_copy(bins_all, bins_smem, smem_sem)
    smem_copy.start()

    @pl.loop(0, my_pos)
    def _(i):
        pos_copy(i, i).wait_recv()
        keep_block(i)

    @pl.loop(my_pos + 1, npos)
    def _(i):
        pos_copy(i, i).wait_recv()
        keep_block(i)

    smem_copy.wait()
    d_one, d_two = dil_ref[0], dil_ref[1]

    def gather(part, to):
        tiles = []
        for b in range(CUT) if part == 0 else range(CUT, 5):
            for v in range(VARS):
                at = bins_smem[to, v] + (MARGIN + (b - 2) * d_two)
                for a in range(5):
                    stage[b * 5 + a, pl.ds(v, 1), :] = padded[pl.ds(at + (a - 2) * d_one, 1), :]
            tiles += fold([stage[b * 5 + a] for a in range(4)], width, wide_lane)
            tiles.append(stage[b * 5 + 4])
        return jnp.concatenate(tiles, axis=0).astype(jnp.bfloat16)

    def part_rows(part):
        return slice(0, CUT * TILES * VARS) if part == 0 else slice(CUT * TILES * VARS, 5 * TILES * VARS)

    for part in range(2):

        @pl.loop(1, nvar)
        def _(i):
            to = lax.rem(my_var + i, nvar)
            send[to, part_rows(part), :] = gather(part, to)
            var_copy(part, to, my_var).start()

        recv[my_var, part_rows(part), :] = gather(part, my_var)

    for load in loads[3:]:
        load.wait()
    shape = (VARS, chans)
    codes = pick([codes_ref[v] for v in range(VARS)], (VARS, 1))
    centre = pick([bins_ref[v] for v in range(VARS)], (VARS, 1))
    changes = []
    for strand in range(2):
        change = jnp.zeros(shape, jnp.float32)
        for code in range(4):
            row = embed_ref[pl.ds(code if strand == 0 else 3 - code, 1), :]
            change = jnp.where(codes == code, row, change)
        changes.append(change)

    def taps_of(layer, strand):
        order = (0, 1, 2) if strand == 0 else (2, 1, 0)
        return [taps_ref[t, pl.ds(layer, 1), :] for t in order]

    def put(at, pair):
        where = pl.ds(pl.multiple_of(at * 16, 16), 16)
        feature[where, :] = jnp.concatenate(pair, axis=0).astype(jnp.bfloat16)

    gain_one = gain_ref[0:1, :]
    step = STEP if chans % STEP == 0 else 128

    def arrive(part):
        @pl.loop(1, nvar)
        def _(i):
            other = lax.rem(my_var + i, nvar)
            var_copy(part, other, other).wait_recv()

    def reference_rows(low, high):
        @pl.loop(low, high)
        def _(b):
            slabs = [[] for _ in range(5)]
            at = pl.ds(pl.multiple_of(b * TILES * VARS, 16), TILES * VARS)
            for j in range(nvar):
                tiles = recv[j, at, :].astype(jnp.float32)
                tiles = [tiles[VARS * k : VARS * (k + 1)] for k in range(TILES)]
                for a, slab in enumerate(unfold(tiles[:3], width, wide_lane) + [tiles[3]]):
                    slabs[a].append(slab[:, :width])
            for a in range(5):
                rows_x[b * 5 + a] = jnp.concatenate(slabs[a], axis=-1)

        @pl.loop(low, high)
        def _(b):
            for a in range(3):
                pair = []
                for strand in range(2):
                    taps = taps_of(0, strand)
                    conv = (
                        taps[0] * rows_x[b * 5 + a]
                        + taps[1] * rows_x[b * 5 + a + 1]
                        + taps[2] * rows_x[b * 5 + a + 2]
                    )
                    pair.append(gelu_of_norm(conv, gain_one))
                put(b * 3 + a, pair)

    def project(low, high):
        @pl.loop(0, chans // step)
        def _(n):
            cols = pl.ds(pl.multiple_of(n * step, step), step)
            first[low:high, cols] = jnp.dot(
                feature[low:high, :], w_one[:, cols], preferred_element_type=jnp.float32
            )

    arrive(0)
    reference_rows(0, CUT)
    load_one.wait()
    project(0, CUT * 48)
    arrive(1)
    reference_rows(CUT, 5)
    for a in range(3):
        pair = []
        for strand in range(2):
            taps = taps_of(0, strand)
            xs = [rows_x[10 + a + t] for t in range(3)]
            xs[2 - a] = xs[2 - a] + changes[strand]
            pair.append(gelu_of_norm(taps[0] * xs[0] + taps[1] * xs[1] + taps[2] * xs[2], gain_one))
        put(15 + a, pair)
    project(CUT * 48, 18 * 16)

    def inside(a, b):
        at = centre + (a - 1) * d_one + (b - 2) * d_two
        return (at >= 0) & (at < bins)

    def rounded(value, keep):
        return jnp.where(keep, value, 0.0).astype(jnp.bfloat16).astype(jnp.float32)

    @pl.loop(0, 5)
    def _(b):
        for a in range(3):
            keep = inside(a, b)
            for strand in range(2):
                at = pl.ds(pl.multiple_of((b * 3 + a) * 16 + 8 * strand, 8), 8)
                first[at, :] = rounded(rows_x[b * 5 + a + 1] + first[at, :], keep)

    for a in range(3):
        keep = inside(a, 2)
        for strand in range(2):
            at = pl.ds((15 + a) * 16 + 8 * strand, 8)
            middle = rows_x[11 + a]
            if a == 1:
                middle = middle + changes[strand]
            first[at, :] = rounded(middle + first[at, :], keep)

    same = d_one == d_two
    total = jnp.zeros(shape, jnp.float32)
    moved = jnp.zeros(shape, jnp.float32)
    gain = gain_ref[1:2, :]
    if True:
        for strand in range(2):
            taps = taps_of(1, strand)

            def ref_at(a, b):
                return first[pl.ds((b * 3 + a) * 16 + 8 * strand, 8), :]

            def new_at(a):
                return first[pl.ds((15 + a) * 16 + 8 * strand, 8), :]

            def alt_at(a, b):
                if b == 2:
                    return new_at(a)
                if b > 2 and a + b - 2 <= 2:
                    return jnp.where(same, new_at(a + b - 2), ref_at(a, b))
                return ref_at(a, b)

            for a in range(3):
                for b in range(1, 4):
                    weight = inside(a, b).astype(jnp.float32)
                    if (a, b) in ((1, 1), (1, 2), (2, 1), (2, 2)):
                        weight = jnp.where(same, 0.0, weight)
                    olds = [ref_at(a, b + t) for t in (-1, 0, 1)]
                    news = [alt_at(a, b + t) for t in (-1, 0, 1)]
                    old, new = (
                        gelu_of_norm(taps[0] * r[0] + taps[1] * r[1] + taps[2] * r[2], gain)
                        .astype(jnp.bfloat16)
                        .astype(jnp.float32)
                        for r in (olds, news)
                    )
                    total = total + weight * (new - old)
                    if b >= 2:
                        moved = moved + weight * (news[1] - olds[1])

    high = total.astype(jnp.bfloat16)
    low = (total - high.astype(jnp.float32)).astype(jnp.bfloat16)
    feature[pl.ds(0, 16), :] = jnp.concatenate(
        [high.astype(jnp.float32), low.astype(jnp.float32)], axis=0
    ).astype(jnp.bfloat16)
    out_ref[...] = moved
    load_two.wait()

    if True:
        @pl.loop(0, chans // step)
        def _(n):
            cols = pl.ds(pl.multiple_of(n * step, step), step)
            both = jnp.dot(
                feature[pl.ds(0, 16), :], w_two[:, cols], preferred_element_type=jnp.float32
            )
            out_ref[:, cols] = (out_ref[:, cols] + (both[:8] + both[8:])) * (0.5 / CONE)

    @pl.loop(1, nvar)
    def _(i):
        other = lax.rem(my_var + i, nvar)
        bin_copy(other, my_var).wait_send()
        var_copy(0, other, my_var).wait_send()
        var_copy(1, other, my_var).wait_send()

    @pl.loop(1, npos)
    def _(i):
        pos_copy(lax.rem(my_pos + i, npos), my_pos).wait_send()


def solution(mesh):
    npos, nvar = mesh.shape["pos"], mesh.shape["var"]

    def local(tower, var_bins, alt_codes, dilations, base_embed, dw_kernel, norm_gain, pw_weight):
        block, width = tower.shape
        chans = pw_weight.shape[1]
        bins = npos * block
        taps = jnp.transpose(dw_kernel, (1, 0, 2))
        vmem = pl.BlockSpec(memory_space=pltpu.VMEM)
        dma = pltpu.SemaphoreType.DMA
        return pl.pallas_call(
            functools.partial(kernel, npos, nvar),
            out_shape=jax.ShapeDtypeStruct((VARS, chans), jnp.float32),
            in_specs=[pl.BlockSpec(memory_space=pltpu.HBM)] * 8,
            out_specs=vmem,
            scratch_shapes=[
                pltpu.SMEM((VARS,), jnp.int32),
                pltpu.SMEM((VARS,), jnp.int32),
                pltpu.SMEM((2,), jnp.int32),
                pltpu.VMEM((block, width), jnp.bfloat16),
                pltpu.VMEM(base_embed.shape, jnp.float32),
                pltpu.VMEM((3, 2, chans), jnp.float32),
                pltpu.VMEM((2, chans), jnp.float32),
                pltpu.VMEM((chans, chans), jnp.bfloat16),
                pltpu.VMEM((chans, chans), jnp.bfloat16),
                pltpu.VMEM((block * 3 // 4, 128), jnp.bfloat16),
                pltpu.VMEM((npos, block * 3 // 4, 128), jnp.bfloat16),
                pltpu.VMEM((bins + 2 * MARGIN, 128), jnp.float32),
                pltpu.VMEM((1, 128), jnp.int32),
                pltpu.VMEM((nvar, 128), jnp.int32),
                pltpu.SMEM((nvar, 128), jnp.int32),
                pltpu.VMEM((25, VARS, 128), jnp.float32),
                pltpu.VMEM((nvar, 5 * TILES * VARS, 128), jnp.bfloat16),
                pltpu.VMEM((nvar, 5 * TILES * VARS, 128), jnp.bfloat16),
                pltpu.VMEM((25, VARS, chans), jnp.float32),
                pltpu.VMEM((18 * 16, chans), jnp.bfloat16),
                pltpu.VMEM((18 * 16, chans), jnp.float32),
                dma((7,)),
                dma((2,)),
                dma((npos,)),
                dma((npos,)),
                dma((nvar,)),
                dma((nvar,)),
                dma((2, nvar)),
                dma((2, nvar)),
                dma,
                pltpu.SemaphoreType.REGULAR((npos,)),
            ],
            compiler_params=pltpu.CompilerParams(
                collective_id=0, has_side_effects=True, vmem_limit_bytes=60 * 1024 * 1024
            ),
        )(var_bins, alt_codes, dilations, tower, base_embed, taps, norm_gain, pw_weight)

    in_specs = (P("pos", "var"), P(("pos", "var")), P(("pos", "var")), P(), P(), P(), P(), P())
    return jax.shard_map(
        local, mesh=mesh, in_specs=in_specs, out_specs=P(("pos", "var"), None), check_vma=False
    )
```

time: 46.3 us -> 36.9 us (0.80); the launches traced: 45.6 us -> 36.7 us
  Pallas kernels: 40 us -> 35.3 us
  local copies, waits for them, and re-layouts: 5.52 us -> 1.42 us
    pallas_call x1, Pallas kernels: 40 us -> 35.3 us  [local(): pl.pallas_call(functools.partial(kernel, npos, nvar), out_shape=jax.Shape...]
    unnamed x14 -> x1, local copies, waits for them, and re-layouts: 5.52 us -> 1.42 us
where the time goes in v2:
time: 36.9 us; the launch traced here: 36.7 us
  Pallas kernels  35.3 us (96%)
  local copies, waits for them, and re-layouts  1.42 us (4%)
    pallas_call x1, Pallas kernels, local(): pl.pallas_call(functools.partial(kernel, npos, nvar), out_shape=jax.Shape...  35.3 us
    unnamed x1, local copies, waits for them, and re-layouts  1.42 us

profile of v2, /device:TPU:1, one launch (start us, length us, event | category | flops | bytes accessed | tf_op | source)
XLA Modules:
  0.0 36.7 jit_solution(3698543378824859082)
XLA Ops:
  0.0 35.3 %shard_map.82 = f32[8,1536]{1,0:T(8,128)} custom-call(s32[8]{0:T(128)} %bins_hbm.1, s32[8]{0:T(128)} %codes_hbm.1, s32[2]{0:T(128)} %dil_hbm.1, bf16[64,96]{1,0:T(8,128)(2,1)} %tower_hbm.1, f32[4,1536]{1,0:T(4,128)} %embed_hbm.1, f32[3,2,1536]{2,1,0:T(2,128)} %bitcast.1, f32[2,1536]{1,0:T(2,128)} %gain_hbm.1, bf16[2,1536,1536]{2,1,0:T(8,128)(2,1)} %weight_ref.1), custom_call_target="tpu_custom_call" | custom-call | tf_op jit(solution)/shard_map/pallas_call | solution.py:438
  35.3 1.4 %copy.10 = f32[8,1536]{1,0:T(8,128)} copy(f32[8,1536]{1,0:T(8,128)} %shard_map.82) | data formatting | bytes 98304

commit v3 on v2

v3 whole, which is shorter than its diff:
```python
import functools

import jax
import jax.numpy as jnp
from jax import lax
from jax.experimental import pallas as pl
from jax.experimental.pallas import tpu as pltpu
from jax.sharding import PartitionSpec as P

DMAX = 7
CONE = 32
VARS = 8
MARGIN = 32
TILES = 4
PARTS = ((0, 3), (3, 5))
MESH = pl.DeviceIdType.MESH
STEP = 1536


CHUNK = 256


def gelu(normed):
    inner = normed * (0.7978845608028654 + (0.7978845608028654 * 0.044715) * (normed * normed))
    half = 0.5 * normed
    return half + half * jnp.tanh(inner)


def pick(scalars, shape):
    row = lax.broadcasted_iota(jnp.int32, shape, len(shape) - 2)
    value = jnp.full(shape, scalars[0], jnp.int32)
    for v in range(1, VARS):
        value = jnp.where(row == v, scalars[v], value)
    return value


def fold(rows, width, lane):
    return [
        jnp.where(lane < width, rows[k], pltpu.roll(rows[3], width - 32 * k, 1)) for k in range(3)
    ]


def unfold(three, width, lane):
    moved = [pltpu.roll(three[k], 128 - width + 32 * k, 1) for k in range(3)]
    last = jnp.where(lane < 64, moved[1], moved[2])
    return list(three) + [jnp.where(lane < 32, moved[0], last)]


def kernel(
    npos,
    nvar,
    bins_hbm,
    codes_hbm,
    dil_hbm,
    tower_hbm,
    embed_hbm,
    taps_hbm,
    gain_hbm,
    weight_ref,
    out_ref,
    bins_ref,
    codes_ref,
    dil_ref,
    tower_ref,
    embed_ref,
    taps_ref,
    gain_ref,
    w_one,
    w_two,
    packed,
    field,
    padded,
    bins_row,
    bins_all,
    bins_smem,
    stage,
    send,
    recv,
    rows_x,
    conv,
    feature,
    first,
    total,
    change,
    in_sem,
    w_sem,
    pos_send,
    pass_send,
    pos_recv,
    bin_send,
    bin_recv,
    var_send,
    var_recv,
    smem_sem,
    ready,
):
    block, width = tower_ref.shape
    bins = npos * block
    chans = out_ref.shape[1]
    my_pos = lax.axis_index("pos")
    my_var = lax.axis_index("var")

    pairs = (
        (tower_hbm, tower_ref),
        (bins_hbm, bins_ref),
        (dil_hbm, dil_ref),
        (codes_hbm, codes_ref),
        (embed_hbm, embed_ref),
        (taps_hbm, taps_ref),
        (gain_hbm, gain_ref),
    )
    loads = [pltpu.make_async_copy(s, d, in_sem.at[i]) for i, (s, d) in enumerate(pairs)]
    for load in loads:
        load.start()
    barrier = pltpu.get_barrier_semaphore()

    length, half = npos // 2, npos // 4
    my_z, my_side = lax.div(my_pos, 2), lax.rem(my_pos, 2)
    partner = my_pos + 1 - 2 * my_side

    def along(z):
        return 2 * z + my_side

    @pl.loop(my_z + 1, length)
    def _(z):
        pl.semaphore_signal(barrier, inc=1, device_id=(along(z), my_var), device_id_type=MESH)

    @pl.when(my_side == 0)
    def _():
        pl.semaphore_signal(barrier, inc=1, device_id=(partner, my_var), device_id_type=MESH)

    @pl.loop(my_var + 1, nvar)
    def _(i):
        pl.semaphore_signal(barrier, inc=1, device_id=(my_pos, i), device_id_type=MESH)

    load_one = pltpu.make_async_copy(weight_ref.at[0], w_one, w_sem.at[0])
    load_two = pltpu.make_async_copy(weight_ref.at[1], w_two, w_sem.at[1])
    load_one.start()
    load_two.start()

    def bin_copy(to, slot):
        return pltpu.make_async_remote_copy(
            src_ref=bins_row,
            dst_ref=bins_all.at[pl.ds(slot, 1)],
            send_sem=bin_send.at[to],
            recv_sem=bin_recv.at[slot],
            device_id=(my_pos, to),
            device_id_type=MESH,
        )

    def pos_copy(to, slot):
        return pltpu.make_async_remote_copy(
            src_ref=packed,
            dst_ref=field.at[slot],
            send_sem=pos_send.at[to],
            recv_sem=pos_recv.at[slot],
            device_id=(to, my_var),
            device_id_type=MESH,
        )

    def pass_on(slot):
        return pltpu.make_async_remote_copy(
            src_ref=field.at[slot],
            dst_ref=field.at[slot],
            send_sem=pass_send.at[slot],
            recv_sem=pos_recv.at[slot],
            device_id=(partner, my_var),
            device_id_type=MESH,
        )

    def var_copy(part, to, slot):
        low, high = PARTS[part]
        at = pl.ds(low * TILES * VARS, (high - low) * TILES * VARS)
        return pltpu.make_async_remote_copy(
            src_ref=send.at[to, at],
            dst_ref=recv.at[slot, at],
            send_sem=var_send.at[part, to],
            recv_sem=var_recv.at[part, slot],
            device_id=(my_pos, to),
            device_id_type=MESH,
        )

    wide_lane = lax.broadcasted_iota(jnp.int32, (VARS, 128), 1)
    two_lane = lax.broadcasted_iota(jnp.int32, (16, 128), 1)
    loads[0].wait()
    own = jnp.concatenate(
        [tower_ref[...].astype(jnp.float32), jnp.zeros((block, 128 - width), jnp.float32)], axis=-1
    )
    quarter = block // 4
    folded = fold([own[quarter * k : quarter * (k + 1)] for k in range(4)], width, two_lane)
    packed[...] = jnp.concatenate(folded, axis=0).astype(jnp.bfloat16)
    loads[1].wait()
    lane = lax.broadcasted_iota(jnp.int32, (1, 128), 1)
    line = jnp.zeros((1, 128), jnp.int32)
    for v in range(VARS):
        line = jnp.where(lane == v, bins_ref[v], line)
    bins_row[...] = line
    bins_all[pl.ds(my_var, 1), :] = line

    heard = my_z + my_side + my_var

    @pl.when(heard > 0)
    def _():
        pl.semaphore_wait(barrier, heard)

    def say(to):
        pl.semaphore_signal(ready.at[my_pos], inc=1, device_id=(to, my_var), device_id_type=MESH)

    @pl.loop(0, my_z)
    def _(z):
        say(along(z))

    @pl.loop(0, my_z)
    def _(z):
        pos_copy(along(z), my_pos).start()

    @pl.when(my_side == 1)
    def _():
        say(partner)
        pos_copy(partner, my_pos).start()

    @pl.loop(0, my_var)
    def _(i):
        bin_copy(i, my_var).start()

    padded[:MARGIN, :] = jnp.zeros((MARGIN, 128), jnp.float32)
    padded[MARGIN + bins :, :] = jnp.zeros((MARGIN, 128), jnp.float32)
    padded[pl.ds(pl.multiple_of(MARGIN + my_pos * block, 8), block), :] = own

    def keep_block(i):
        three = field[i].astype(jnp.float32)
        four = unfold([three[quarter * k : quarter * (k + 1)] for k in range(3)], width, two_lane)
        for k in range(4):
            at = pl.multiple_of(MARGIN + i * block + quarter * k, 8)
            padded[pl.ds(at, quarter), :] = four[k]

    loads[2].wait()

    def answer(low, high):
        @pl.loop(low, high)
        def _(z):
            pl.semaphore_wait(ready.at[along(z)], 1)
            pos_copy(along(z), my_pos).start()

    def take(low, high):
        @pl.loop(low, high)
        def _(z):
            pos_copy(along(z), along(z)).wait_recv()
            pass_on(along(z)).start()
            keep_block(along(z))

    @pl.when(my_z < half)
    def _():
        answer(my_z + 1, half)

    @pl.when(my_z >= half)
    def _():
        answer(my_z + 1, length)

    @pl.when(my_side == 0)
    def _():
        pl.semaphore_wait(ready.at[partner], 1)
        pos_copy(partner, my_pos).start()

    def answer_bins():
        @pl.loop(my_var + 1, nvar)
        def _(i):
            bin_copy(i, i).wait_recv()
            bin_copy(i, my_var).start()

    @pl.when(my_z < half)
    def _():
        take(0, my_z)
        take(my_z + 1, half)
        answer(half, length)
        answer_bins()
        take(half, length)

    @pl.when(my_z >= half)
    def _():
        answer_bins()
        take(0, half)
        take(half, my_z)
        take(my_z + 1, length)

    @pl.loop(0, my_var)
    def _(i):
        bin_copy(i, i).wait_recv()

    smem_copy = pltpu.make_async_copy(bins_all, bins_smem, smem_sem)
    smem_copy.start()

    @pl.loop(0, length)
    def _(z):
        other = 2 * z + 1 - my_side
        pos_copy(other, other).wait_recv()
        keep_block(other)

    smem_copy.wait()
    d_one, d_two = dil_ref[0], dil_ref[1]

    def gather(part, to):
        tiles = []
        for b in range(*PARTS[part]):
            for v in range(VARS):
                at = bins_smem[to, v] + (MARGIN + (b - 2) * d_two)
                for a in range(5):
                    stage[b * 5 + a, pl.ds(v, 1), :] = padded[pl.ds(at + (a - 2) * d_one, 1), :]
            tiles += fold([stage[b * 5 + a] for a in range(4)], width, wide_lane)
            tiles.append(stage[b * 5 + 4])
        return jnp.concatenate(tiles, axis=0).astype(jnp.bfloat16)

    for part, (low, high) in enumerate(PARTS):
        rows = slice(low * TILES * VARS, high * TILES * VARS)

        @pl.loop(1, nvar)
        def _(i):
            to = lax.rem(my_var + i, nvar)
            send[to, rows, :] = gather(part, to)
            var_copy(part, to, my_var).start()

        recv[my_var, rows, :] = gather(part, my_var)

    for load in loads[3:]:
        load.wait()
    shape = (VARS, chans)
    codes = pick([codes_ref[v] for v in range(VARS)], (VARS, 1))
    centre = pick([bins_ref[v] for v in range(VARS)], (VARS, 1))
    for strand in range(2):
        value = jnp.zeros(shape, jnp.float32)
        for code in range(4):
            row = embed_ref[pl.ds(code if strand == 0 else 3 - code, 1), :]
            value = jnp.where(codes == code, row, value)
        change[strand] = value

    chunks = [slice(k, k + CHUNK) for k in range(0, chans, CHUNK)]
    step = STEP if chans % STEP == 0 else 128
    steps = chans // step

    def arrive(part):
        @pl.loop(1, nvar)
        def _(i):
            other = lax.rem(my_var + i, nvar)
            var_copy(part, other, other).wait_recv()

    def assemble(b):
        slabs = [[] for _ in range(5)]
        at = pl.ds(pl.multiple_of(b * TILES * VARS, 16), TILES * VARS)
        for j in range(nvar):
            tiles = recv[j, at, :].astype(jnp.float32)
            tiles = [tiles[VARS * k : VARS * (k + 1)] for k in range(TILES)]
            for a, slab in enumerate(unfold(tiles[:3], width, wide_lane) + [tiles[3]]):
                slabs[a].append(slab[:, :width])
        for a in range(5):
            rows_x[b * 5 + a] = jnp.concatenate(slabs[a], axis=-1)

    def scales(squares):
        return [lax.rsqrt(jnp.sum(s, axis=-1, keepdims=True) / chans + 1e-06) for s in squares]

    def halves(value):
        return sum(value[:, k : k + 128] for k in range(0, value.shape[1], 128))

    def layer_one(at, xs_of):
        squares = [0.0] * 6
        for cols in chunks:
            taps = [taps_ref[t, 0:1, cols] for t in range(3)]
            for k, value in enumerate(xs_of(cols, taps)):
                conv[k, :, cols] = value
                squares[k] = squares[k] + halves(value * value)
        scale = scales(squares)
        for cols in chunks:
            gain = gain_ref[0:1, cols]
            for a in range(3):
                pair = [gelu(conv[2 * a + s, :, cols] * scale[2 * a + s] * gain) for s in range(2)]
                where = pl.ds(pl.multiple_of((at + a) * 16, 16), 16)
                feature[where, cols] = jnp.concatenate(pair, axis=0).astype(jnp.bfloat16)

    def reference_rows(b):
        def xs_of(cols, taps):
            xs = [rows_x[b * 5 + a, :, cols] for a in range(5)]
            low, high = [taps[0] * x for x in xs], [taps[2] * x for x in xs]
            out = []
            for a in range(3):
                middle = taps[1] * xs[a + 1]
                out += [low[a] + middle + high[a + 2], high[a] + middle + low[a + 2]]
            return out

        layer_one(b * 3, xs_of)

    def alternate_rows():
        def xs_of(cols, taps):
            out = []
            for a in range(3):
                for strand in range(2):
                    xs = [rows_x[10 + a + t, :, cols] for t in range(3)]
                    xs[2 - a] = xs[2 - a] + change[strand, :, cols]
                    first, last = (taps[0], taps[2]) if strand == 0 else (taps[2], taps[0])
                    out.append(first * xs[0] + taps[1] * xs[1] + last * xs[2])
            return out

        layer_one(15, xs_of)

    def project(low, high):
        @pl.loop(0, steps)
        def _(n):
            cols = pl.ds(pl.multiple_of(n * step, step), step)
            first[low:high, cols] = jnp.dot(
                feature[low:high, :], w_one[:, cols], preferred_element_type=jnp.float32
            )

    def inside(a, b):
        at = centre + (a - 1) * d_one + (b - 2) * d_two
        return (at >= 0) & (at < bins)

    def finish(block, middle, keep):
        for strand in range(2):
            at = pl.ds(pl.multiple_of(block * 16 + 8 * strand, 8), 8)
            value = jnp.where(keep, middle(strand) + first[at, :], 0.0)
            first[at, :] = value.astype(jnp.bfloat16).astype(jnp.float32)

    same = d_one == d_two

    def layer_two(a, b, with_moved):
        weight = inside(a, b).astype(jnp.float32)
        if b <= 2:
            weight = jnp.where(same & (a >= 1), 0.0, weight)

        def ref_at(b, strand, cols):
            at = pl.multiple_of((b * 3 + a) * 16 + 8 * strand, 8)
            return first[pl.ds(at, 8), cols]

        def new_at(a, strand, cols):
            at = pl.multiple_of((15 + a) * 16 + 8 * strand, 8)
            return first[pl.ds(at, 8), cols]

        def both(strand, cols):
            olds = [ref_at(b + t, strand, cols) for t in (-1, 0, 1)]
            news = list(olds)
            for t in range(3):
                at = b + t - 1
                if at == 2:
                    news[t] = new_at(a, strand, cols)
                elif at > 2:
                    other = new_at(jnp.minimum(a + at - 2, 2), strand, cols)
                    news[t] = jnp.where(same & (a + at - 2 <= 2), other, olds[t])
            return olds, news

        squares = [0.0] * 4
        for cols in chunks:
            taps = [taps_ref[t, 1:2, cols] for t in range(3)]
            for strand in range(2):
                order = taps if strand == 0 else taps[::-1]
                olds, news = both(strand, cols)
                if b >= 2:
                    moved = weight * (news[1] - olds[1])
                    out_ref[:, cols] = out_ref[:, cols] + moved
                old = [k * x for k, x in zip(order, olds)]
                new = [p if x is y else k * y for k, p, x, y in zip(order, old, olds, news)]
                for k, (p, q, r) in enumerate((old, new)):
                    value = p + q + r
                    conv[2 * strand + k, :, cols] = value
                    squares[2 * strand + k] = squares[2 * strand + k] + halves(value * value)
        scale = scales(squares)
        for cols in chunks:
            gain = gain_ref[1:2, cols]
            sums = total[:, cols]
            for strand in range(2):
                old, new = (
                    gelu(conv[2 * strand + k, :, cols] * scale[2 * strand + k] * gain)
                    .astype(jnp.bfloat16)
                    .astype(jnp.float32)
                    for k in range(2)
                )
                sums = sums + weight * (new - old)
            total[:, cols] = sums

    total[...] = jnp.zeros_like(total)
    out_ref[...] = jnp.zeros_like(out_ref)

    arrive(0)

    @pl.loop(0, 3)
    def _(b):
        assemble(b)
        reference_rows(b)

    alternate_rows()
    arrive(1)

    @pl.loop(3, 5)
    def _(b):
        assemble(b)
        reference_rows(b)

    load_one.wait()
    project(0, 18 * 16)

    @pl.loop(0, 5)
    def _(b):
        for a in range(3):
            finish(b * 3 + a, lambda strand: rows_x[b * 5 + a + 1], inside(a, b))

    for a in range(3):
        extra = (lambda strand: change[strand]) if a == 1 else (lambda strand: 0.0)
        finish(15 + a, lambda strand: rows_x[11 + a] + extra(strand), inside(a, 2))

    @pl.loop(0, 3)
    def _(a):
        for b in range(1, 4):
            layer_two(a, b, b > 1)

    high = total[...].astype(jnp.bfloat16)
    low = (total[...] - high.astype(jnp.float32)).astype(jnp.bfloat16)
    feature[pl.ds(0, 16), :] = jnp.concatenate(
        [high.astype(jnp.float32), low.astype(jnp.float32)], axis=0
    ).astype(jnp.bfloat16)
    load_two.wait()

    @pl.loop(0, steps)
    def _(n):
        cols = pl.ds(pl.multiple_of(n * step, step), step)
        both = jnp.dot(
            feature[pl.ds(0, 16), :], w_two[:, cols], preferred_element_type=jnp.float32
        )
        out_ref[:, cols] = (out_ref[:, cols] + (both[:8] + both[8:])) * (0.5 / CONE)

    @pl.loop(1, nvar)
    def _(i):
        other = lax.rem(my_var + i, nvar)
        bin_copy(other, my_var).wait_send()
        for part in range(len(PARTS)):
            var_copy(part, other, my_var).wait_send()

    pos_copy(partner, my_pos).wait_send()

    @pl.loop(1, length)
    def _(i):
        to = along(lax.rem(my_z + i, length))
        pos_copy(to, my_pos).wait_send()
        pass_on(to).wait_send()


def solution(mesh):
    npos, nvar = mesh.shape["pos"], mesh.shape["var"]

    def local(tower, var_bins, alt_codes, dilations, base_embed, dw_kernel, norm_gain, pw_weight):
        block, width = tower.shape
        chans = pw_weight.shape[1]
        bins = npos * block
        taps = jnp.transpose(dw_kernel, (1, 0, 2))
        vmem = pl.BlockSpec(memory_space=pltpu.VMEM)
        dma = pltpu.SemaphoreType.DMA
        return pl.pallas_call(
            functools.partial(kernel, npos, nvar),
            out_shape=jax.ShapeDtypeStruct((VARS, chans), jnp.float32),
            in_specs=[pl.BlockSpec(memory_space=pltpu.HBM)] * 8,
            out_specs=vmem,
            scratch_shapes=[
                pltpu.SMEM((VARS,), jnp.int32),
                pltpu.SMEM((VARS,), jnp.int32),
                pltpu.SMEM((2,), jnp.int32),
                pltpu.VMEM((block, width), jnp.bfloat16),
                pltpu.VMEM(base_embed.shape, jnp.float32),
                pltpu.VMEM((3, 2, chans), jnp.float32),
                pltpu.VMEM((2, chans), jnp.float32),
                pltpu.VMEM((chans, chans), jnp.bfloat16),
                pltpu.VMEM((chans, chans), jnp.bfloat16),
                pltpu.VMEM((block * 3 // 4, 128), jnp.bfloat16),
                pltpu.VMEM((npos, block * 3 // 4, 128), jnp.bfloat16),
                pltpu.VMEM((bins + 2 * MARGIN, 128), jnp.float32),
                pltpu.VMEM((1, 128), jnp.int32),
                pltpu.VMEM((nvar, 128), jnp.int32),
                pltpu.SMEM((nvar, 128), jnp.int32),
                pltpu.VMEM((25, VARS, 128), jnp.float32),
                pltpu.VMEM((nvar, 5 * TILES * VARS, 128), jnp.bfloat16),
                pltpu.VMEM((nvar, 5 * TILES * VARS, 128), jnp.bfloat16),
                pltpu.VMEM((25, VARS, chans), jnp.float32),
                pltpu.VMEM((6, VARS, chans), jnp.float32),
                pltpu.VMEM((18 * 16, chans), jnp.bfloat16),
                pltpu.VMEM((18 * 16, chans), jnp.float32),
                pltpu.VMEM((VARS, chans), jnp.float32),
                pltpu.VMEM((2, VARS, chans), jnp.float32),
                dma((7,)),
                dma((2,)),
                dma((npos,)),
                dma((npos,)),
                dma((npos,)),
                dma((nvar,)),
                dma((nvar,)),
                dma((3, nvar)),
                dma((3, nvar)),
                dma,
                pltpu.SemaphoreType.REGULAR((npos,)),
            ],
            compiler_params=pltpu.CompilerParams(
                collective_id=0, has_side_effects=True, vmem_limit_bytes=60 * 1024 * 1024
            ),
        )(var_bins, alt_codes, dilations, tower, base_embed, taps, norm_gain, pw_weight)

    in_specs = (P("pos", "var"), P(("pos", "var")), P(("pos", "var")), P(), P(), P(), P(), P())
    return jax.shard_map(
        local, mesh=mesh, in_specs=in_specs, out_specs=P(("pos", "var"), None), check_vma=False
    )
```

time: 36.9 us -> 36.2 us (0.981)
  Pallas kernels: 35.3 us -> 34.6 us
    pallas_call x1, Pallas kernels: 35.3 us -> 34.6 us  [local(): pl.pallas_call(functools.partial(kernel, npos, nvar), out_shape=jax.Shape...]
where the time goes in v3:
time: 36.2 us; the launch traced here: 36.1 us
  Pallas kernels  34.6 us (96%)
  local copies, waits for them, and re-layouts  1.42 us (4%)
    pallas_call x1, Pallas kernels, local(): pl.pallas_call(functools.partial(kernel, npos, nvar), out_shape=jax.Shape...  34.6 us
    unnamed x1, local copies, waits for them, and re-layouts  1.42 us

profile of v3, /device:TPU:1, one launch (start us, length us, event | category | flops | bytes accessed | tf_op | source)
XLA Modules:
  0.0 36.1 jit_solution(16078684668841210503)
XLA Ops:
  0.0 34.6 %shard_map.82 = f32[8,1536]{1,0:T(8,128)} custom-call(s32[8]{0:T(128)} %bins_hbm.1, s32[8]{0:T(128)} %codes_hbm.1, s32[2]{0:T(128)} %dil_hbm.1, bf16[64,96]{1,0:T(8,128)(2,1)} %tower_hbm.1, f32[4,1536]{1,0:T(4,128)} %embed_hbm.1, f32[3,2,1536]{2,1,0:T(2,128)} %bitcast.1, f32[2,1536]{1,0:T(2,128)} %gain_hbm.1, bf16[2,1536,1536]{2,1,0:T(8,128)(2,1)} %weight_ref.1), custom_call_target="tpu_custom_call" | custom-call | tf_op jit(solution)/shard_map/pallas_call | solution.py:553
  34.6 1.4 %copy.10 = f32[8,1536]{1,0:T(8,128)} copy(f32[8,1536]{1,0:T(8,128)} %shard_map.82) | data formatting | bytes 98304

commit v4 on v3

--- a/solution.py
+++ b/solution.py
@@ -552,7 +552,7 @@
         dma = pltpu.SemaphoreType.DMA
         return pl.pallas_call(
             functools.partial(kernel, npos, nvar),
-            out_shape=jax.ShapeDtypeStruct((VARS, chans), jnp.float32),
+            out_shape=pltpu.VMEM((VARS, chans), jnp.float32),
             in_specs=[pl.BlockSpec(memory_space=pltpu.HBM)] * 8,
             out_specs=vmem,
             scratch_shapes=[

time: 36.2 us -> 34.8 us (0.961)
  local copies, waits for them, and re-layouts: 1.42 us -> 0.62 us
  Pallas kernels: 34.6 us -> 34 us
    unnamed x1, local copies, waits for them, and re-layouts: 1.42 us -> 0.62 us
    pallas_call x1, Pallas kernels: 34.6 us -> 34 us  [local(): pl.pallas_call(functools.partial(kernel, npos, nvar), out_shape=pltpu.VME...]
where the time goes in v4:
time: 34.8 us; the launch traced here: 34.6 us
  Pallas kernels  34 us (98%)
  local copies, waits for them, and re-layouts  0.62 us (2%)
    pallas_call x1, Pallas kernels, local(): pl.pallas_call(functools.partial(kernel, npos, nvar), out_shape=pltpu.VME...  34 us

profile of v4, /device:TPU:1, one launch (start us, length us, event | category | flops | bytes accessed | tf_op | source)
XLA Modules:
  0.0 34.6 jit_solution(14724587499648854384)
XLA Ops:
  0.0 34.0 %shard_map.82 = f32[8,1536]{1,0:T(8,128)S(1)} custom-call(s32[8]{0:T(128)} %bins_hbm.1, s32[8]{0:T(128)} %codes_hbm.1, s32[2]{0:T(128)} %dil_hbm.1, bf16[64,96]{1,0:T(8,128)(2,1)} %tower_hbm.1, f32[4,1536]{1,0:T(4,128)} %embed_hbm.1, f32[3,2,1536]{2,1,0:T(2,128)} %bitcast.1, f32[2,1536]{1,0:T(2,128)} %gain_hbm.1, bf16[2,1536,1536]{2,1,0:T(8,128)(2,1)} %weight_ref.1), custom_call_target="tpu_custom_call" | custom-call | tf_op jit(solution)/shard_map/pallas_call | solution.py:553
  34.0 0.6 %copy.10 = f32[8,1536]{1,0:T(8,128)} copy(f32[8,1536]{1,0:T(8,128)S(1)} %shard_map.82) | data formatting | bytes 98304

commit v5 on v4

--- a/solution.py
+++ b/solution.py
@@ -247,6 +247,9 @@
         def _(z):
             pos_copy(along(z), along(z)).wait_recv()
             pass_on(along(z)).start()
+
+        @pl.loop(low, high)
+        def _(z):
             keep_block(along(z))
 
     @pl.when(my_z < half)
@@ -315,7 +318,7 @@
 
         @pl.loop(1, nvar)
         def _(i):
-            to = lax.rem(my_var + i, nvar)
+            to = lax.rem(my_var + 3 * i, nvar)
             send[to, rows, :] = gather(part, to)
             var_copy(part, to, my_var).start()
 

time: 34.8 us -> 33.7 us (0.968)
  Pallas kernels: 34 us -> 32.9 us
    pallas_call x1, Pallas kernels: 34 us -> 32.9 us  [local(): pl.pallas_call(functools.partial(kernel, npos, nvar), out_shape=pltpu.VME...]
where the time goes in v5:
time: 33.7 us; the launch traced here: 33.5 us
  Pallas kernels  32.9 us (98%)
  local copies, waits for them, and re-layouts  0.62 us (2%)
    pallas_call x1, Pallas kernels, local(): pl.pallas_call(functools.partial(kernel, npos, nvar), out_shape=pltpu.VME...  32.9 us

profile of v5, /device:TPU:1, one launch (start us, length us, event | category | flops | bytes accessed | tf_op | source)
XLA Modules:
  0.0 33.5 jit_solution(8819984730696163018)
XLA Ops:
  0.0 32.9 %shard_map.82 = f32[8,1536]{1,0:T(8,128)S(1)} custom-call(s32[8]{0:T(128)} %bins_hbm.1, s32[8]{0:T(128)} %codes_hbm.1, s32[2]{0:T(128)} %dil_hbm.1, bf16[64,96]{1,0:T(8,128)(2,1)} %tower_hbm.1, f32[4,1536]{1,0:T(4,128)} %embed_hbm.1, f32[3,2,1536]{2,1,0:T(2,128)} %bitcast.1, f32[2,1536]{1,0:T(2,128)} %gain_hbm.1, bf16[2,1536,1536]{2,1,0:T(8,128)(2,1)} %weight_ref.1), custom_call_target="tpu_custom_call" | custom-call | tf_op jit(solution)/shard_map/pallas_call | solution.py:556
  32.9 0.6 %copy.10 = f32[8,1536]{1,0:T(8,128)} copy(f32[8,1536]{1,0:T(8,128)S(1)} %shard_map.82) | data formatting | bytes 98304
